TPU v7x, 128 devices: a whole 4x4x4 slice. The times are simulated.
128 devices in a mesh: group: 8 (over z, x_hi), tensor: 16 (over x_lo, y, core).
Axes of the slice: x: 4 (x_hi: 2, x_lo: 2; x = x_hi * 2 + x_lo), y: 4, z: 4, core: 2. Of those that a mesh axis runs over, the one named last changes fastest.
Arguments:
- frozen_base_matrix: bfloat16 [5120, 25600], P(None, 'tensor'), may hold values from -0.078125 to 0.078125
- master_a: float32 [64, 16, 320], P(None, 'tensor', 'group'), may hold values from -0.03125 to 0.03125
- moment1_a: float32 [64, 16, 320], P(None, 'tensor', 'group'), may hold values from -120 to 120
- moment2_a: float32 [64, 16, 320], P(None, 'tensor', 'group'), may hold values from 16 to 500
- master_b: float32 [64, 16, 1600], P(None, 'tensor', 'group'), may hold values from -1.2 to 1.2
- moment1_b: float32 [64, 16, 1600], P(None, 'tensor', 'group'), may hold values from -1.2 to 1.2
- moment2_b: float32 [64, 16, 1600], P(None, 'tensor', 'group'), may hold values from 0.002 to 0.06
- learner_token_inputs: bfloat16 [4096, 5120], P('group', 'tensor'), may hold values from -6 to 6
- learner_output_cotangents: bfloat16 [4096, 25600], P('group', 'tensor'), may hold values from -0.29882812 to 0.29882812
- rollout_inputs: bfloat16 [4096, 5120], P(('group', 'tensor')), may hold values from -6 to 6
Outputs:
- rollout_out: bfloat16 [4096, 25600], P('group', 'tensor')
- master_a_next: float32 [64, 16, 320], P(None, 'tensor', 'group')
- moment1_a_next: float32 [64, 16, 320], P(None, 'tensor', 'group')
- moment2_a_next: float32 [64, 16, 320], P(None, 'tensor', 'group')
- master_b_next: float32 [64, 16, 1600], P(None, 'tensor', 'group')
- moment1_b_next: float32 [64, 16, 1600], P(None, 'tensor', 'group')
- moment2_b_next: float32 [64, 16, 1600], P(None, 'tensor', 'group')
All inputs are finite; a program needn't handle non-finite values.
Results may differ from a plain program's by a relative error of at most 0.006.
Values may be sent and summed in bfloat16 or wider, within the bound.
A program may use at most 128 MiB of HBM per device.

v0:
```python
import jax
import jax.numpy as jnp
from jax import lax
from jax.sharding import PartitionSpec as P

beta_one = 0.9
beta_two = 0.999
learn_rate = 0.001
adam_eps = 1e-08
adapter_scale = 2.0
fix_one = 0.9999734386011124
fix_two = 0.0952078528862904


def adam_step(master, first, second, grad):
    first_next = beta_one * first + (1.0 - beta_one) * grad
    second_next = beta_two * second + (1.0 - beta_two) * grad * grad
    master_next = master - learn_rate * (first_next / fix_one) / (
        jnp.sqrt(second_next / fix_two) + adam_eps
    )
    return (master_next, first_next, second_next)


def contract_dims(left, right, left_dim, right_dim):
    return lax.dot_general(
        left, right, (((left_dim,), (right_dim,)), ((), ())), preferred_element_type=jnp.float32
    )


def shards(
    frozen_base_matrix,
    master_a,
    moment1_a,
    moment2_a,
    master_b,
    moment1_b,
    moment2_b,
    learner_token_inputs,
    learner_output_cotangents,
    rollout_inputs,
):
    old_a, old_b = (
        lax.all_gather(master_a.astype(jnp.bfloat16), "group", axis=2, tiled=True),
        lax.all_gather(master_b.astype(jnp.bfloat16), "group", axis=2, tiled=True),
    )
    a_rows = old_a[:, 0, :]
    b_cols = old_b[:, 0, :]
    hidden_part = contract_dims(learner_token_inputs, a_rows, 1, 1)
    back_part = contract_dims(learner_output_cotangents, b_cols, 1, 1)
    hidden_sum, back_sum = lax.psum((hidden_part, back_part), "tensor")
    hidden_lowrank = hidden_sum.astype(jnp.bfloat16)
    backward_lowrank = back_sum.astype(jnp.bfloat16)
    down_factor_gradient = adapter_scale * contract_dims(
        backward_lowrank, learner_token_inputs, 0, 0
    )
    up_factor_gradient = adapter_scale * contract_dims(
        hidden_lowrank, learner_output_cotangents, 0, 0
    )
    width_a = master_a.shape[2]
    width_b = master_b.shape[2]
    total_a, total_b = lax.psum((down_factor_gradient, up_factor_gradient), "group")
    offset = lax.axis_index("group")
    share_a = lax.dynamic_slice_in_dim(total_a, offset * width_a, width_a, 1)
    share_b = lax.dynamic_slice_in_dim(total_b, offset * width_b, width_b, 1)
    master_a_next, moment1_a_next, moment2_a_next = adam_step(
        master_a, moment1_a, moment2_a, share_a[:, None, :]
    )
    master_b_next, moment1_b_next, moment2_b_next = adam_step(
        master_b, moment1_b, moment2_b, share_b[:, None, :]
    )
    new_a = master_a_next.astype(jnp.bfloat16)
    new_b = master_b_next.astype(jnp.bfloat16)
    ranks = new_a.shape[0]
    rows_group, cols_group = (
        lax.all_gather(new_a, "group", axis=2, tiled=True),
        lax.all_gather(new_b, "group", axis=2, tiled=True),
    )
    complete_down_factor = lax.all_gather(rows_group, "tensor", axis=1, tiled=True).reshape(
        ranks, -1
    )
    column_span = cols_group[:, 0, :]
    merged_weight_matrix = (
        frozen_base_matrix.astype(jnp.float32)
        + adapter_scale * contract_dims(complete_down_factor, column_span, 0, 0)
    ).astype(jnp.bfloat16)
    rollout_out = jnp.dot(
        lax.all_gather(rollout_inputs, "tensor", axis=0, tiled=True),
        merged_weight_matrix,
        preferred_element_type=jnp.float32,
    ).astype(jnp.bfloat16)
    return (
        rollout_out,
        master_a_next,
        moment1_a_next,
        moment2_a_next,
        master_b_next,
        moment1_b_next,
        moment2_b_next,
    )


def solution(mesh):
    return jax.shard_map(
        shards,
        mesh=mesh,
        in_specs=(
            P(None, "tensor"),
            P(None, "tensor", "group"),
            P(None, "tensor", "group"),
            P(None, "tensor", "group"),
            P(None, "tensor", "group"),
            P(None, "tensor", "group"),
            P(None, "tensor", "group"),
            P("group", "tensor"),
            P("group", "tensor"),
            P(("group", "tensor"), None),
        ),
        out_specs=(
            P("group", "tensor"),
            P(None, "tensor", "group"),
            P(None, "tensor", "group"),
            P(None, "tensor", "group"),
            P(None, "tensor", "group"),
            P(None, "tensor", "group"),
            P(None, "tensor", "group"),
        ),
        check_vma=False,
    )
```

profile of v0, /device:TPU:1, one launch (start us, length us, event | category | flops | bytes accessed | tf_op | source)
XLA Modules:
  0.0 369.0 jit_solution(17257363519027183208)
XLA Ops:
  8.0 0.0 copy-start
  8.1 0.0 all-reduce.5.cloned.1.call-start
  8.1 0.9 convert_element_type.34
  9.0 0.8 copy.65
  9.8 0.1 copy.45
  10.0 30.4 %all_gather.21 = bf16[64,1,320]{0,2,1:T(8,128)(2,1)S(1)} all-gather(bf16[64,1,40]{0,2,1:T(8,128)(2,1)S(1)} %convert_element_type.34), channel_id=1, replica_groups=mesh['group'=8,'tensor'=16] {'group'}, dimensions={2}, use_global_device_ids=true | all-gather | bytes 46080 | tf_op jit(solution)/shard_map/all_gather | solution.py:43
  40.4 1.2 fusion.7
  41.6 32.5 %all_gather.18 = bf16[64,1,1600]{0,1,2:T(2,128)(2,1)S(1)} all-gather(bf16[64,1,200]{0,1,2:T(2,128)(2,1)S(1)} %copy.45), channel_id=1, replica_groups=mesh['group'=8,'tensor'=16] {'group'}, dimensions={2}, use_global_device_ids=true | all-gather | bytes 230400 | tf_op jit(solution)/shard_map/all_gather | solution.py:44
  74.1 1.1 copy.46
  75.2 0.4 fusion.5
  75.6 62.1 %all-reduce.6 = (bf16[512,64]{0,1:T(8,128)(2,1)S(1)}, bf16[512,64]{0,1:T(8,128)(2,1)S(1)}) all-reduce(f32[512,64]{0,1:T(8,128)S(1)} %fusion.5, f32[512,64]{0,1:T(8,128)S(1)} %fusion.7), channel_id=1, replica_groups=mesh['group'=8,'tensor'=16] {'tensor'}, use_global_device_ids=true, to_apply=%region_0.0 | all-reduce | flops 65536 | bytes 393216 | tf_op jit(solution)/shard_map/psum | solution.py:50
  137.7 0.9 convolution_multiply_fusion.1
  138.6 1.4 convolution_multiply_fusion
  140.0 0.0 all-reduce.5.cloned.1.call-update
  140.0 0.0 all-gather.2.cloned.1.call-start
  140.1 0.5 all-gather.2.cloned.1.call-update
  140.6 95.6 %all-reduce.5.cloned.1.call-done = (f32[64,320]{0,1:T(8,128)}, f32[64,1600]{1,0:T(8,128)}) async-done(((f32[64,320]{0,1:T(8,128)}, f32[64,1600]{1,0:T(8,128)}), (f32[64,320]{0,1:T(8,128)}, f32[64,1600]{1,0:T(8,128)})) %all-reduce.5.cloned.1.call-update) | async-done | bytes 491536 | tf_op jit(solution)/shard_map/psum | solution.py:61
  236.2 1.4 fusion.18
  237.6 28.2 %all_gather.19 = bf16[64,1,320]{0,2,1:T(8,128)(2,1)S(1)} all-gather(bf16[64,1,40]{0,2,1:T(8,128)(2,1)S(1)} %get-tuple-element.43), channel_id=1, replica_groups=mesh['group'=8,'tensor'=16] {'group'}, dimensions={2}, use_global_device_ids=true | all-gather | bytes 46080 | tf_op jit(solution)/shard_map/all_gather | solution.py:75
  265.8 0.1 copy.47
  265.9 1.0 fusion.16
  266.9 0.7 copy.54
  267.6 0.7 copy.55
  268.3 0.7 copy.56
  269.0 0.1 copy.52
  269.2 31.9 %all_gather.22 = bf16[64,1,1600]{0,1,2:T(2,128)(2,1)S(1)} all-gather(bf16[64,1,200]{0,1,2:T(2,128)(2,1)S(1)} %copy.52), channel_id=1, replica_groups=mesh['group'=8,'tensor'=16] {'group'}, dimensions={2}, use_global_device_ids=true | all-gather | bytes 230400 | tf_op jit(solution)/shard_map/all_gather | solution.py:76
  301.1 1.1 copy.53
  302.2 37.2 %all_gather.20 = bf16[64,16,320]{2,0,1:T(8,128)(2,1)S(1)} all-gather(bf16[64,1,320]{2,0,1:T(8,128)(2,1)S(1)} %copy.47), channel_id=1, replica_groups=mesh['group'=8,'tensor'=16] {'tensor'}, dimensions={1}, use_global_device_ids=true | all-gather | bytes 696320 | tf_op jit(solution)/shard_map/all_gather | solution.py:78
  339.3 0.5 copy.48
  339.8 0.6 reshape.23
  340.4 0.0 all-gather.2.cloned.1.call-done
  340.5 21.0 %fusion.2 = bf16[512,1600]{0,1:T(8,128)(2,1)} fusion(bf16[512,5120]{1,0:T(8,128)(2,1)} %all-gather.2.cloned.1.call-done, bf16[5120,1600]{0,1:T(8,128)(2,1)} %param.10, bf16[64,5120]{1,0:T(8,128)(2,1)S(1)} %reshape.23, bf16[64,1,1600]{2,0,1:T(8,128)(2,1)S(1)} %copy.53), kind=kOutput, calls=%fused_computation.3 | convolution fusion | flops 9470771200 | bytes 24125440 | tf_op jit(solution)/shard_map/dot_general | solution.py:86
  (15 shorter events, 0.0 us)
Async XLA Ops:
  8.0 67.1 %copy-start = (bf16[512,1600]{0,1:T(8,128)(2,1)S(1)}, bf16[512,1600]{0,1:T(8,128)(2,1)}, u32[]{:S(2)}) copy-start(bf16[512,1600]{0,1:T(8,128)(2,1)} %param.18) | copy-start | bytes 4915204
  8.0 228.2 %copy-start.3 = (f32[64,1,40]{0,2,1:T(8,128)S(1)}, f32[64,1,40]{0,2,1:T(8,128)}, u32[]{:S(2)}) copy-start(f32[64,1,40]{0,2,1:T(8,128)} %param.11) | copy-start | bytes 30724
  8.0 257.9 %copy-start.2 = (f32[64,1,200]{2,1,0:T(1,128)S(1)}, f32[64,1,200]{2,1,0:T(1,128)}, u32[]{:S(2)}) copy-start(f32[64,1,200]{2,1,0:T(1,128)} %param.14) | copy-start | bytes 153604
  8.0 129.7 %copy-start.1 = (bf16[512,320]{0,1:T(8,128)(2,1)S(1)}, bf16[512,320]{0,1:T(8,128)(2,1)}, u32[]{:S(2)}) copy-start(bf16[512,320]{0,1:T(8,128)(2,1)} %param.17) | copy-start | bytes 983044
  8.1 228.2 %copy-start.7 = (f32[64,1,40]{0,2,1:T(8,128)S(1)}, f32[64,1,40]{0,2,1:T(8,128)}, u32[]{:S(2)}) copy-start(f32[64,1,40]{0,2,1:T(8,128)} %param.13) | copy-start | bytes 30724
  8.1 228.2 %copy-start.6 = (f32[64,1,40]{0,2,1:T(8,128)S(1)}, f32[64,1,40]{0,2,1:T(8,128)}, u32[]{:S(2)}) copy-start(f32[64,1,40]{0,2,1:T(8,128)} %param.12) | copy-start | bytes 30724
  8.1 257.8 %copy-start.5 = (f32[64,1,200]{2,1,0:T(1,128)S(1)}, f32[64,1,200]{2,1,0:T(1,128)}, u32[]{:S(2)}) copy-start(f32[64,1,200]{2,1,0:T(1,128)} %param.16) | copy-start | bytes 153604
  8.1 257.8 %copy-start.4 = (f32[64,1,200]{2,1,0:T(1,128)S(1)}, f32[64,1,200]{2,1,0:T(1,128)}, u32[]{:S(2)}) copy-start(f32[64,1,200]{2,1,0:T(1,128)} %param.15) | copy-start | bytes 153604
  8.1 228.1 %all-reduce.5.cloned.1.call-start = ((), (), s32[]{:S(2)}) async-start(), calls=%async_computation.1 | async-start | bytes 1179648 | tf_op jit(solution)/shard_map/psum | solution.py:61
  140.0 200.4 %all-gather.2.cloned.1.call-start = ((), (), s32[]{:S(2)}) async-start(), calls=%async_computation | async-start | bytes 5570560 | tf_op jit(solution)/shard_map/all_gather | solution.py:87
Sparse Core Ops, SparseCore 0:
  140.1 96.0 all-reduce.4
Sparse Core Ops, SparseCore 1:
  142.2 48.5 all-gather.1
where the time goes:
time: 369 us
  blocking collectives  222 us (60%)
  waiting for transfers between devices  96.2 us (26%)
  matrix products  24.9 us (7%)
  between operations  15.7 us (4%)
  local copies, waits for them, and re-layouts  6.52 us (2%)
    psum x1, waiting for transfers between devices, shards(): lax.psum((down_factor_gradient, up_factor_gradient), 'group')  95.6 us
    psum x1, blocking collectives, shards(): hidden_sum, back_sum = lax.psum((hidden_part, back_part), 'tensor')  62.1 us
    all_gather x1, blocking collectives, shards(): lax.all_gather(rows_group, 'tensor', axis=1, tiled=True).reshape(ranks, -1)  37.2 us
    all_gather x1, blocking collectives, shards(): lax.all_gather(master_b.astype(jnp.bfloat16), 'group', axis=2, tiled=True)  32.5 us
    all_gather x1, blocking collectives, shards(): lax.all_gather(new_b, 'group', axis=2, tiled=True)  31.9 us
    all_gather x1, blocking collectives, shards(): lax.all_gather(master_a.astype(jnp.bfloat16), 'group', axis=2, tiled=True)  30.4 us
    all_gather x1, blocking collectives, shards(): lax.all_gather(new_a, 'group', axis=2, tiled=True)  28.2 us
    dot_general x1, matrix products, shards(): jnp.dot(lax.all_gather(rollout_inputs, 'tensor', axis=0, tiled=True), mer...  21 us
  transfers between devices with their start and end apart: 2, of which 1 were waited for; matrix products, arithmetic and copies ran while one was open for 2% of the time, Pallas kernels for 0%

commit v1 on v0

v1 whole, which is shorter than its diff:
```python
import functools

import jax
import jax.numpy as jnp
from jax import lax
from jax.experimental import pallas as pl
from jax.experimental.pallas import tpu as pltpu
from jax.sharding import PartitionSpec as P

beta_one = 0.9
beta_two = 0.999
learn_rate = 0.001
adam_eps = 1e-08
adapter_scale = 2.0
fix_one = 0.9999734386011124
fix_two = 0.0952078528862904

MESH = pl.DeviceIdType.MESH
BF = jnp.bfloat16
F32 = jnp.float32

D, HID, TOK, COLS, ROWS = 5120, 1600, 512, 320, 32
SHARE_A, SHARE_B, RANK = 40, 200, 64
NT, NG = 16, 8

TENSOR_STEPS = sorted(
    ((dx, dy, dc) for dx in range(2) for dy in range(4) for dc in range(2) if (dx, dy, dc) != (0, 0, 0)),
    key=lambda s: -(s[0] + min(s[1], 4 - s[1]) + 0.1 * s[2]),
)
GROUP_STEPS = sorted(
    ((dz, dx) for dz in range(4) for dx in range(2) if (dz, dx) != (0, 0)),
    key=lambda s: -(min(s[0], 4 - s[0]) + 2 * s[1]),
)


def dot(left, right, left_dim, right_dim):
    return lax.dot_general(
        left, right, (((left_dim,), (right_dim,)), ((), ())), preferred_element_type=F32
    )


def aligned(index, size):
    return pl.ds(pl.multiple_of(index * size, size), size)


def kernel(
    base_hbm, ma_hbm, m1a_hbm, m2a_hbm, mb_hbm, m1b_hbm, m2b_hbm, xt_hbm, cot_hbm, xr_hbm,
    out_hbm, ma_out, m1a_out, m2a_out, mb_out, m1b_out, m2b_out,
    base, xt, cot, xall, acc, out_v, a_in, b_in, pad, msg0, got0, msg0b, mom_a, mom_b,
    old_a, old_b, part, got1, low, own2, grad_b, grad_a, msg3, got3, stats, msg4, got4, b_rows, b_left, b_right,
    a_left, a_right, part5, got5, own5, xa, b_out,
    loc, s0, r0, s0b, r0b, s1, r1, s2, r2, s3, r3, s4, r4, s5, r5, s6, r6, sx, rx, sc, rc,
):
    g = lax.axis_index("group")
    t = lax.axis_index("tensor")
    z, far = g // 2, lax.rem(g, 2)
    xl, y, core = t // 8, lax.rem(t // 2, 4), lax.rem(t, 2)

    def tensor_at(dx, dy, dc):
        return lax.rem(xl + dx, 2) * 8 + lax.rem(y + dy, 4) * 2 + lax.rem(core + dc, 2)

    def group_at(dz, dx):
        return lax.rem(z + dz, 4) * 2 + lax.rem(far + dx, 2)

    tensor_peers = [tensor_at(*s) for s in TENSOR_STEPS]
    group_peers = [group_at(*s) for s in GROUP_STEPS]

    def remote(src, dst, ssem, rsem, k, gg, tt):
        copy = pltpu.make_async_remote_copy(
            src_ref=src, dst_ref=dst, send_sem=ssem.at[k], recv_sem=rsem.at[k],
            device_id=(gg, tt), device_id_type=MESH,
        )
        copy.start()
        return copy

    sent = []

    def load(src, dst, k):
        copy = pltpu.make_async_copy(src, dst, loc.at[k])
        copy.start()
        return copy

    loads_b = [load(ref, b_in.at[i], i) for i, ref in enumerate((mb_hbm, m1b_hbm, m2b_hbm))]
    loads_a = [load(ref, a_in.at[i], 3 + i) for i, ref in enumerate((ma_hbm, m1a_hbm, m2a_hbm))]
    mine = aligned(t, ROWS)
    load_x = load(xr_hbm, xall.at[mine], 6)
    load_cot = load(cot_hbm, cot, 7)
    load_xt = load(xt_hbm, xt, 8)
    load_base = load(base_hbm, base, 9)

    bar = pltpu.get_barrier_semaphore()
    for gg in group_peers:
        pl.semaphore_signal(bar, inc=1, device_id=(gg, t), device_id_type=MESH)
    for tt in tensor_peers:
        pl.semaphore_signal(bar, inc=1, device_id=(g, tt), device_id_type=MESH)

    pad[...] = jnp.zeros_like(pad)
    for copy in loads_b + loads_a:
        copy.wait()
    pad[0, 0:SHARE_A, 0:RANK] = a_in[0]
    factor_a = pad[0].T[0:RANK, 0:SHARE_A]
    msg0[...] = jnp.zeros_like(msg0)
    msg0[:, 0:SHARE_B] = b_in[0, :, 0, :].astype(BF)
    msg0[:, SHARE_B:SHARE_B + SHARE_A] = factor_a.astype(BF)
    got0[g] = msg0[...]
    pl.semaphore_wait(bar, len(group_peers) + len(tensor_peers))

    copies0 = [remote(msg0, got0.at[g], s0, r0, k, gg, t) for k, gg in enumerate(group_peers)]

    x_next, y_up, y_down, sibling = tensor_at(1, 0, 0), tensor_at(0, 1, 0), tensor_at(0, 3, 0), tensor_at(0, 0, 1)
    half = D // 2
    low_half, high_half, all_of = pl.ds(0, half), pl.ds(half, half), pl.ds(0, D)

    def send_x(owner, columns, k, to):
        where = xall.at[aligned(owner, ROWS), columns]
        return remote(where, where, sx, rx, k, g, to)

    def share_x(owner, k):
        where = xall.at[aligned(owner, ROWS)]
        return remote(where, where, sc, rc, k, g, sibling)

    load_x.wait()
    step1 = [send_x(t, all_of, 0, x_next), send_x(t, all_of, 1, y_up), send_x(t, all_of, 2, y_down)]
    shared = [share_x(t, 0)]

    msg0b[...] = jnp.zeros_like(msg0b)
    msg0b[0, :, 0:RANK] = a_in[1]
    msg0b[0, :, RANK:2 * RANK] = a_in[0]
    msg0b[1, :, RANK:2 * RANK] = a_in[2]
    rows_a = aligned(g, SHARE_A)
    mom_a[:, rows_a, :] = msg0b[...]
    copies0b = [
        remote(msg0b, mom_a.at[:, rows_a, :], s0b, r0b, k, gg, t) for k, gg in enumerate(group_peers)
    ]

    mom_b[...] = jnp.zeros_like(mom_b)
    for i in range(3):
        pad[1, 0:RANK, 0:128] = b_in[i, :, 0, 0:128]
        pad[2, 0:RANK, 0:SHARE_B - 128] = b_in[i, :, 0, 128:SHARE_B]
        mom_b[i, 0:128, :] = pad[1].T
        mom_b[i, 128:256, :] = pad[2].T
    a_left[...] = jnp.zeros_like(a_left)
    a_right[...] = jnp.zeros_like(a_right)
    grad_b[HID:HID + 8, :] = jnp.zeros((8, 128), F32)

    for copy in copies0:
        copy.wait_recv()
    for j in range(NG):
        old_b[:, j * SHARE_B:(j + 1) * SHARE_B] = got0[j, :, 0:SHARE_B]
        old_a[:, j * SHARE_A:(j + 1) * SHARE_A] = got0[j, :, SHARE_B:SHARE_B + SHARE_A]
    load_cot.wait()
    load_xt.wait()
    hidden = dot(old_a[...], xt[...], 1, 0)
    back = dot(old_b[...], cot[...], 1, 0)
    for h in range(2):
        part[h, 0:RANK, :] = hidden[:, h * 256:(h + 1) * 256].astype(BF)
        part[h, RANK:, :] = back[:, h * 256:(h + 1) * 256].astype(BF)
    copies1 = [
        remote(part.at[lax.rem(tt, 2), aligned(tt // 2, 16)], got1.at[k], s1, r1, k, g, tt)
        for k, tt in enumerate(tensor_peers)
    ]

    for copy in step1:
        copy.wait_recv()
    of_x, of_up, of_down = x_next, y_up, y_down
    step2 = [
        send_x(of_up, low_half, 3, x_next),
        send_x(of_down, low_half, 4, x_next),
        send_x(of_x, high_half, 5, y_up),
        send_x(of_x, high_half, 6, y_down),
        send_x(of_down, low_half, 7, y_up),
        send_x(of_up, high_half, 8, y_down),
    ]
    shared += [share_x(of_x, 1), share_x(of_up, 2), share_x(of_down, 3)]

    for copy in copies1:
        copy.wait_recv()
    my_half, my_rows = lax.rem(t, 2), aligned(t // 2, 16)
    total = part[my_half, my_rows, :].astype(F32)
    for k in range(NT - 1):
        total = total + got1[k].astype(F32)
    own2[...] = total.astype(BF)
    low[my_half, my_rows, :] = own2[...]
    copies2 = [
        remote(own2, low.at[my_half, my_rows], s2, r2, k, g, tt) for k, tt in enumerate(tensor_peers)
    ]
    for copy in copies2:
        copy.wait_recv()

    low0, low1 = low[0], low[1]
    grad_a[...] = dot(xt[:, 0:256], low0, 1, 1) + dot(xt[:, 256:512], low1, 1, 1)

    def grad_rows(i, carry):
        rows = aligned(i, 400)
        grad_b[rows, :] = dot(cot[rows, 0:256], low0, 1, 1) + dot(cot[rows, 256:512], low1, 1, 1)
        return carry

    lax.fori_loop(0, HID // 400, grad_rows, 0)
    lanes = lax.broadcasted_iota(jnp.int32, (COLS, 128), 1)
    left = lanes < RANK

    def message3(j):
        rows = pl.ds(pl.multiple_of(j * SHARE_B, 8), 208)
        return jnp.where(left[0:208], grad_b[rows, :], grad_a[0:208, :]).astype(BF)

    rest = grad_a[208:COLS, :].astype(BF)
    copies3 = []
    for k, gg in enumerate(group_peers):
        msg3[k, 0:208, :] = message3(gg)
        msg3[k, 208:COLS, :] = rest
        copies3.append(remote(msg3.at[k], got3.at[g], s3, r3, k, gg, t))
    got3[g, 0:208, :] = message3(g)
    got3[g, 208:COLS, :] = rest

    for copy in step2:
        copy.wait_recv()
    across = tensor_at(0, 2, 0)
    quarter = D // 4
    step3 = [
        send_x(across, low_half, 9, x_next),
        send_x(tensor_at(1, 1, 0), pl.ds(2 * quarter, quarter), 10, y_down),
        send_x(tensor_at(1, 3, 0), pl.ds(3 * quarter, quarter), 11, y_up),
    ]
    shared += [share_x(across, 4), share_x(tensor_at(1, 1, 0), 5), share_x(tensor_at(1, 3, 0), 6)]

    def base_rows(h, first, last):
        tokens = aligned(h, 256)

        def body(i, carry):
            rows = aligned(i, 800)
            acc[h, rows, :] = dot(base[rows, :], xall[tokens, :], 1, 1)
            return carry

        lax.fori_loop(first, last, body, 0)

    load_base.wait()
    for k in (0, 2, 3, 4):
        shared[k].wait_recv()
    base_rows(xl, 0, 2)

    for copy in copies0b:
        copy.wait_recv()
    for copy in copies3:
        copy.wait_recv()
    grad = got3[0].astype(F32)
    for j in range(1, NG):
        grad = grad + got3[j].astype(F32)
    grad = adapter_scale * grad
    master = jnp.where(left, mom_b[0], mom_a[0])
    first = jnp.where(left, mom_b[1], pltpu.roll(mom_a[0], RANK, 1))
    second = jnp.where(left, mom_b[2], mom_a[1])
    first_next = beta_one * first + (1.0 - beta_one) * grad
    second_next = beta_two * second + (1.0 - beta_two) * grad * grad
    master_next = master - learn_rate * (first_next / fix_one) / (
        jnp.sqrt(second_next / fix_two) + adam_eps
    )
    stats[0] = master_next
    stats[1] = first_next
    stats[2] = second_next
    factors = master_next.astype(BF).astype(F32)
    only_a = jnp.where(left, 0.0, factors)
    place = pl.ds(pl.multiple_of(core * RANK, RANK), COLS)
    a_right[place, :] = only_a.astype(BF)
    a_left[place, :] = pltpu.roll(only_a, RANK, 1).astype(BF)
    msg4[...] = jnp.where(left[0:208], factors[0:208], 0.0).astype(BF)
    got4[g] = msg4[...]
    copies4 = [remote(msg4, got4.at[g], s4, r4, k, gg, t) for k, gg in enumerate(group_peers)]

    for copy in step3:
        copy.wait_recv()
    shared.append(share_x(tensor_at(1, 2, 0), 7))
    for k in (1, 5, 6, 7):
        shared[k].wait_recv()
    window = pl.ds(pl.multiple_of((t // 2) * 640 + core * 256, 128), 384)
    part5[...] = (
        dot(xall[0:256, window], a_left[...], 1, 0) + dot(xall[256:512, window], a_right[...], 1, 0)
    ).astype(BF)
    copies5 = [
        remote(part5.at[aligned(tt, 16)], got5.at[k], s5, r5, k, g, tt)
        for k, tt in enumerate(tensor_peers)
    ]

    base_rows(1 - xl, 0, 1)

    for copy in copies5:
        copy.wait_recv()
    mine5 = aligned(t, 16)
    total = part5[mine5, :].astype(F32)
    for k in range(NT - 1):
        total = total + got5[k].astype(F32)
    own5[...] = (adapter_scale * total).astype(BF)
    xa[mine5, :] = own5[...]
    copies6 = [remote(own5, xa.at[mine5], s6, r6, k, g, tt) for k, tt in enumerate(tensor_peers)]

    base_rows(1 - xl, 1, 2)

    rows_out = aligned(g, SHARE_A)
    for i in range(3):
        a_in[i] = pltpu.roll(stats[i, rows_out, :], RANK, 1)[:, 0:RANK]
        b_out[i, :, 0, 0:128] = stats[i, 0:128, :].T[0:RANK]
        b_out[i, :, 0, 128:SHARE_B] = stats[i, 128:256, :].T[0:RANK, 0:SHARE_B - 128]
    stores = [load(a_in.at[i], ref, 10 + i) for i, ref in enumerate((ma_out, m1a_out, m2a_out))]
    stores += [load(b_out.at[i], ref, 13 + i) for i, ref in enumerate((mb_out, m1b_out, m2b_out))]

    for copy in copies4:
        copy.wait_recv()
    for j in range(NG):
        b_rows[j * SHARE_B:(j + 1) * SHARE_B, :] = got4[j, 0:SHARE_B, :].astype(F32)
    b_left[...] = b_rows[...].astype(BF)
    b_right[...] = pltpu.roll(b_rows[...], RANK, 1).astype(BF)

    for copy in copies6:
        copy.wait_recv()
    for i in range(5):
        rows = pl.ds(320 * i, 320)
        out_v[rows, 0:256] = (acc[0, rows, :] + dot(b_left[rows, :], xa[...], 1, 1)).astype(BF)
        out_v[rows, 256:512] = (acc[1, rows, :] + dot(b_right[rows, :], xa[...], 1, 1)).astype(BF)
        stores.append(load(out_v.at[rows], out_hbm.at[rows], 16 + i))

    for group in (copies0, step1, shared, copies0b, copies1, step2, copies2, copies3, step3, copies4, copies5, copies6):
        for copy in group:
            copy.wait_send()
    for copy in stores:
        copy.wait()


def shards(
    frozen_base_matrix, master_a, moment1_a, moment2_a, master_b, moment1_b, moment2_b,
    learner_token_inputs, learner_output_cotangents, rollout_inputs,
):
    state_a = [ref.reshape(RANK, SHARE_A).T for ref in (master_a, moment1_a, moment2_a)]
    dma = pltpu.SemaphoreType.DMA
    vmem = pltpu.VMEM
    any_space = pl.BlockSpec(memory_space=pl.ANY)
    shape = jax.ShapeDtypeStruct
    results = pl.pallas_call(
        kernel,
        out_shape=[shape((HID, TOK), BF)]
        + [shape((SHARE_A, RANK), F32)] * 3
        + [shape((RANK, 1, SHARE_B), F32)] * 3,
        in_specs=[any_space] * 10,
        out_specs=[any_space] * 7,
        scratch_shapes=[
            vmem((HID, D), BF),
            vmem((COLS, TOK), BF),
            vmem((HID, TOK), BF),
            vmem((TOK, D), BF),
            vmem((2, HID, 256), F32),
            vmem((HID, TOK), BF),
            vmem((3, SHARE_A, RANK), F32),
            vmem((3, RANK, 1, SHARE_B), F32),
            vmem((3, 128, 128), F32),
            vmem((RANK, 256), BF),
            vmem((NG, RANK, 256), BF),
            vmem((2, SHARE_A, 128), F32),
            vmem((2, COLS, 128), F32),
            vmem((3, COLS, 128), F32),
            vmem((RANK, COLS), BF),
            vmem((RANK, HID), BF),
            vmem((2, 128, 256), BF),
            vmem((NT - 1, 16, 256), BF),
            vmem((2, 128, 256), BF),
            vmem((16, 256), BF),
            vmem((HID + 8, 128), F32),
            vmem((COLS, 128), F32),
            vmem((NG - 1, COLS, 128), BF),
            vmem((NG, COLS, 128), BF),
            vmem((3, COLS, 128), F32),
            vmem((208, 128), BF),
            vmem((NG, 208, 128), BF),
            vmem((HID, 128), F32),
            vmem((HID, 128), BF),
            vmem((HID, 128), BF),
            vmem((384, 128), BF),
            vmem((384, 128), BF),
            vmem((256, 128), BF),
            vmem((NT - 1, 16, 128), BF),
            vmem((16, 128), BF),
            vmem((256, 128), BF),
            vmem((3, RANK, 1, SHARE_B), F32),
            dma((24,)),
        ]
        + [dma((n,)) for n in (7, 7, 7, 7, 15, 15, 15, 15, 7, 7, 7, 7, 15, 15, 15, 15, 12, 12, 8, 8)],
        compiler_params=pltpu.CompilerParams(
            collective_id=0, has_side_effects=True, vmem_limit_bytes=56 * 1024 * 1024
        ),
        cost_estimate=pl.CostEstimate(
            flops=2 * TOK * D * HID, bytes_accessed=2 * (D * HID + 3 * TOK * HID), transcendentals=0
        ),
    )(
        frozen_base_matrix.T, *state_a, master_b, moment1_b, moment2_b,
        learner_token_inputs.T, learner_output_cotangents.T, rollout_inputs,
    )
    out, a_next, b_next = results[0], results[1:4], results[4:7]
    return (out.T, *[ref.T.reshape(RANK, 1, SHARE_A) for ref in a_next], *b_next)


def solution(mesh):
    state = P(None, "tensor", "group")
    return jax.shard_map(
        shards,
        mesh=mesh,
        in_specs=(P(None, "tensor"), *[state] * 6, P("group", "tensor"), P("group", "tensor"), P(("group", "tensor"), None)),
        out_specs=(P("group", "tensor"), *[state] * 6),
        check_vma=False,
    )
```

time: 369 us -> 71 us (0.19)
  blocking collectives: 222 us -> 0 us
  waiting for transfers between devices: 96.2 us -> 0 us
  Pallas kernels: 0 us -> 63.7 us
  matrix products: 24.9 us -> 0 us
  between operations: 15.7 us -> 0.7 us
    all_gather x5 -> x0, blocking collectives: 160 us -> none  [the longest x1 37.2 us: shards(): lax.all_gather(rows_group, 'tensor', axis=1, tiled=True).reshape(ranks, -1)]
    psum x1 -> x0, waiting for transfers between devices: 95.6 us -> none  [shards(): lax.psum((down_factor_gradient, up_factor_gradient), 'group')]
    pallas_call x0 -> x1, Pallas kernels: none -> 63.7 us  [shards(): pl.pallas_call(kernel, out_shape=[shape((HID, TOK), BF)] + [shape((SHARE_...]
    psum x1 -> x0, blocking collectives: 62.1 us -> none  [shards(): hidden_sum, back_sum = lax.psum((hidden_part, back_part), 'tensor')]
    dot_general x5 -> x0, matrix products: 24.9 us -> none  [the longest x1 21 us: shards(): jnp.dot(lax.all_gather(rollout_inputs, 'tensor', axis=0, tiled=True), mer...]
  transfers between devices with their start and end apart: 2 -> 0, of which waited for: 1 -> 0; matrix products, arithmetic and copies ran while one was open for 2% -> 0% of each run, Pallas kernels for 0% -> 0%
where the time goes in v1:
time: 71 us; the launch traced here: 70.9 us
  Pallas kernels  63.7 us (90%)
  local copies, waits for them, and re-layouts  6.49 us (9%)
    pallas_call x1, Pallas kernels, shards(): pl.pallas_call(kernel, out_shape=[shape((HID, TOK), BF)] + [shape((SHARE_...  63.7 us
    unnamed x19, local copies, waits for them, and re-layouts  6.49 us

profile of v1, /device:TPU:1, one launch (start us, length us, event | category | flops | bytes accessed | tf_op | source)
XLA Modules:
  0.0 70.9 jit_solution(8554603834955505615)
XLA Ops:
  0.6 63.7 %shard_map.153 = (bf16[1600,512]{1,0:T(8,128)(2,1)}, f32[40,64]{1,0:T(8,128)}, f32[40,64]{1,0:T(8,128)}, f32[40,64]{1,0:T(8,128)}, f32[64,1,200]{2,1,0:T(1,128)}...) custom-call(bf16[1600,5120]{1,0:T(8,128)(2,1)} %bitcast.26, f32[40,64]{1,0:T(8,128)} %bitcast.29, f32[40,64]{1,0:T(8,128)} %bitcast.30, ...), custom_call_target="tpu_custom_call" | custom-call | flops 8388608000 | bytes 21299200 | tf_op jit(solution)/shard_map/pallas_call | solution.py:336
  64.3 0.0 copy-start.5
  64.3 0.0 copy-start.4
  64.3 0.0 copy-start.3
  64.3 0.0 copy-start.2
  64.4 0.0 copy-start.1
  64.4 0.0 copy-start
  64.4 2.8 %copy.24 = bf16[512,1600]{0,1:T(8,128)(2,1)} copy(bf16[512,1600]{0,1:T(8,128)(2,1)} %bitcast.22) | data formatting | bytes 3276800
  67.1 0.0 copy-done.5
  67.1 0.6 copy.25
  67.7 0.0 copy-done.4
  67.7 0.6 copy.26
  68.4 0.0 copy-done.3
  68.4 0.6 copy.27
  69.0 0.0 copy-done.2
  69.0 0.6 copy.28
  69.6 0.0 copy-done.1
  69.6 0.6 copy.29
  70.2 0.0 copy-done
  70.2 0.6 copy.30
Async XLA Ops:
  64.3 2.8 %copy-start.5 = (f32[40,64]{1,0:T(8,128)S(1)}, f32[40,64]{1,0:T(8,128)}, u32[]{:S(2)}) copy-start(f32[40,64]{1,0:T(8,128)} %get-tuple-element.15) | copy-start | bytes 30724
  64.3 3.4 %copy-start.4 = (f32[40,64]{1,0:T(8,128)S(1)}, f32[40,64]{1,0:T(8,128)}, u32[]{:S(2)}) copy-start(f32[40,64]{1,0:T(8,128)} %get-tuple-element.16) | copy-start | bytes 30724
  64.3 4.0 %copy-start.3 = (f32[40,64]{1,0:T(8,128)S(1)}, f32[40,64]{1,0:T(8,128)}, u32[]{:S(2)}) copy-start(f32[40,64]{1,0:T(8,128)} %get-tuple-element.17) | copy-start | bytes 30724
  64.3 4.6 %copy-start.2 = (f32[64,1,200]{2,1,0:T(1,128)S(1)}, f32[64,1,200]{2,1,0:T(1,128)}, u32[]{:S(2)}) copy-start(f32[64,1,200]{2,1,0:T(1,128)} %get-tuple-element.32) | copy-start | bytes 153604
  64.4 5.2 %copy-start.1 = (f32[64,1,200]{2,1,0:T(1,128)S(1)}, f32[64,1,200]{2,1,0:T(1,128)}, u32[]{:S(2)}) copy-start(f32[64,1,200]{2,1,0:T(1,128)} %get-tuple-element.33) | copy-start | bytes 153604
  64.4 5.9 %copy-start = (f32[64,1,200]{2,1,0:T(1,128)S(1)}, f32[64,1,200]{2,1,0:T(1,128)}, u32[]{:S(2)}) copy-start(f32[64,1,200]{2,1,0:T(1,128)} %get-tuple-element.34) | copy-start | bytes 153604

commit v2 on v1

v2 whole, which is shorter than its diff:
```python
import jax
import jax.numpy as jnp
from jax import lax
from jax.experimental import pallas as pl
from jax.experimental.pallas import tpu as pltpu
from jax.sharding import PartitionSpec as P

beta_one = 0.9
beta_two = 0.999
learn_rate = 0.001
adam_eps = 1e-08
adapter_scale = 2.0
fix_one = 0.9999734386011124
fix_two = 0.0952078528862904

MESH = pl.DeviceIdType.MESH
BF = jnp.bfloat16
F32 = jnp.float32

D, HID, TOK, COLS, ROWS = 5120, 1600, 512, 320, 32
SHARE_A, SHARE_B, RANK = 40, 200, 64
NT, NG = 16, 8

TENSOR_STEPS = sorted(
    ((dx, dy, dc) for dx in range(2) for dy in range(4) for dc in range(2) if (dx, dy, dc) != (0, 0, 0)),
    key=lambda s: -(s[0] + min(s[1], 4 - s[1]) + 0.1 * s[2]),
)
GROUP_STEPS = sorted(
    ((dz, dx) for dz in range(4) for dx in range(2) if (dz, dx) != (0, 0)),
    key=lambda s: -(min(s[0], 4 - s[0]) + 2 * s[1]),
)


def dot(left, right, left_dim, right_dim):
    return lax.dot_general(
        left, right, (((left_dim,), (right_dim,)), ((), ())), preferred_element_type=F32
    )


def aligned(index, size):
    return pl.ds(pl.multiple_of(index * size, size), size)


def kernel(
    base_hbm, ma_hbm, m1a_hbm, m2a_hbm, mb_hbm, m1b_hbm, m2b_hbm, xt_hbm, cot_hbm, xr_hbm,
    acc, b_left, b_right, xa, a_state, b_state,
    base, xt, cot, xall, a_in, b_in, pad, msg0, got0, msg0b, mom_a, mom_b,
    old_a, old_b, part, got1, low, own2, grad_b, grad_a, msg3a, got3a, msg3b, got3b, msg4, got4, b_rows, rows_b,
    a_left, a_right, cross, window_x, part5, got5, own5,
    loc, s0, r0, s0b, r0b, s1, r1, s2, r2, s3a, r3a, s3b, r3b, s4, r4, s5, r5, s6, r6, sx, rx, sc, rc, sw, rw,
):
    g = lax.axis_index("group")
    t = lax.axis_index("tensor")
    z, far = g // 2, lax.rem(g, 2)
    xl, y, core = t // 8, lax.rem(t // 2, 4), lax.rem(t, 2)

    def tensor_at(dx, dy, dc):
        return lax.rem(xl + dx, 2) * 8 + lax.rem(y + dy, 4) * 2 + lax.rem(core + dc, 2)

    def group_at(dz, dx):
        return lax.rem(z + dz, 4) * 2 + lax.rem(far + dx, 2)

    tensor_peers = [tensor_at(*s) for s in TENSOR_STEPS]
    group_peers = [group_at(*s) for s in GROUP_STEPS]

    bar = pltpu.get_barrier_semaphore()
    for gg in group_peers:
        pl.semaphore_signal(bar, inc=1, device_id=(gg, t), device_id_type=MESH)
    for tt in tensor_peers:
        pl.semaphore_signal(bar, inc=1, device_id=(g, tt), device_id_type=MESH)

    def remote(src, dst, ssem, rsem, k, gg, tt):
        copy = pltpu.make_async_remote_copy(
            src_ref=src, dst_ref=dst, send_sem=ssem.at[k], recv_sem=rsem.at[k],
            device_id=(gg, tt), device_id_type=MESH,
        )
        copy.start()
        return copy

    def load(src, dst, k):
        copy = pltpu.make_async_copy(src, dst, loc.at[k])
        copy.start()
        return copy

    load_b = load(mb_hbm, b_in.at[0], 0)
    load_a = load(ma_hbm, a_in.at[0], 1)
    mine = aligned(t, ROWS)
    load_x = load(xr_hbm, xall.at[mine], 2)
    load_cot = load(cot_hbm, cot, 3)
    load_xt = load(xt_hbm, xt, 4)
    loads_m = [
        load(m1b_hbm, b_in.at[1], 5), load(m2b_hbm, b_in.at[2], 6),
        load(m1a_hbm, a_in.at[1], 7), load(m2a_hbm, a_in.at[2], 8),
    ]
    load_base = load(base_hbm, base, 9)

    pad[...] = jnp.zeros_like(pad)
    msg0[...] = jnp.zeros_like(msg0)
    load_a.wait()
    pad[0, 0:SHARE_A, 0:RANK] = a_in[0]
    factor_a = pad[0].T[0:RANK, 0:SHARE_A]
    msg0[:, SHARE_B:SHARE_B + SHARE_A] = factor_a.astype(BF)
    load_b.wait()
    msg0[:, 0:SHARE_B] = b_in[0, :, 0, :].astype(BF)
    pl.semaphore_wait(bar, len(group_peers) + len(tensor_peers))
    copies0 = [remote(msg0, got0.at[g], s0, r0, k, gg, t) for k, gg in enumerate(group_peers)]
    got0[g] = msg0[...]

    x_next, y_up, y_down, sibling = tensor_at(1, 0, 0), tensor_at(0, 1, 0), tensor_at(0, 3, 0), tensor_at(0, 0, 1)
    half = D // 2
    low_half, high_half, all_of = pl.ds(0, half), pl.ds(half, half), pl.ds(0, D)

    def send_x(owner, columns, k, to):
        where = xall.at[aligned(owner, ROWS), columns]
        return remote(where, where, sx, rx, k, g, to)

    def share_x(owner, k):
        where = xall.at[aligned(owner, ROWS)]
        return remote(where, where, sc, rc, k, g, sibling)

    def window_of(tt):
        return pl.ds(pl.multiple_of((tt // 2) * 640 + lax.rem(tt, 2) * 256, 128), 384)

    load_x.wait()
    step1 = [send_x(t, all_of, 0, x_next), send_x(t, all_of, 1, y_up), send_x(t, all_of, 2, y_down)]
    shared = [share_x(t, 0)]
    far_chip = [tensor_at(1, 2, 0), tensor_at(1, 2, 1)]
    early = [
        remote(xall.at[mine, window_of(tt)], cross.at[k], sw, rw, k, g, tt) for k, tt in enumerate(far_chip)
    ]

    lanes = lax.broadcasted_iota(jnp.int32, (160, 128), 1)
    left = lanes < RANK

    def beside(first, second):
        rows = first.shape[0]
        return jnp.where(left[0:rows], first, pltpu.roll(second, RANK, 1))

    for copy in loads_m:
        copy.wait()
    for i in range(3):
        pad[1, 0:RANK, 0:128] = b_in[i, :, 0, 0:128]
        pad[2, 0:RANK, 0:SHARE_B - 128] = b_in[i, :, 0, 128:SHARE_B]
        rows_b[0:128, :] = pad[1].T
        rows_b[128:256, :] = pad[2].T
        mom_b[i] = beside(rows_b[0:112, :], rows_b[104:216, :])
    a_left[...] = jnp.zeros_like(a_left)
    a_right[...] = jnp.zeros_like(a_right)
    grad_b[HID:HID + 16, :] = jnp.zeros((16, 128), F32)
    msg0b[...] = jnp.zeros_like(msg0b)
    msg0b[0, :, 0:RANK] = a_in[1]
    msg0b[0, :, RANK:2 * RANK] = a_in[0]
    msg0b[1, :, RANK:2 * RANK] = a_in[2]
    rows_a = aligned(g, SHARE_A)
    mom_a[:, rows_a, :] = msg0b[...]

    for copy in copies0:
        copy.wait_recv()
    for j in range(NG):
        old_b[:, j * SHARE_B:(j + 1) * SHARE_B] = got0[j, :, 0:SHARE_B]
        old_a[:, j * SHARE_A:(j + 1) * SHARE_A] = got0[j, :, SHARE_B:SHARE_B + SHARE_A]
    load_cot.wait()
    load_xt.wait()
    hidden = dot(old_a[...], xt[...], 1, 0)
    back = dot(old_b[...], cot[...], 1, 0)
    for h in range(2):
        part[h, 0:RANK, :] = hidden[:, h * 256:(h + 1) * 256].astype(BF)
        part[h, RANK:, :] = back[:, h * 256:(h + 1) * 256].astype(BF)
    copies1 = [
        remote(part.at[lax.rem(tt, 2), aligned(tt // 2, 16)], got1.at[k], s1, r1, k, g, tt)
        for k, tt in enumerate(tensor_peers)
    ]

    copies0b = [
        remote(msg0b, mom_a.at[:, rows_a, :], s0b, r0b, k, gg, t) for k, gg in enumerate(group_peers)
    ]

    for copy in copies1:
        copy.wait_recv()
    my_half, my_rows = lax.rem(t, 2), aligned(t // 2, 16)
    total = part[my_half, my_rows, :].astype(F32)
    for k in range(NT - 1):
        total = total + got1[k].astype(F32)
    own2[...] = total.astype(BF)
    copies2 = [
        remote(own2, low.at[my_half, my_rows], s2, r2, k, g, tt) for k, tt in enumerate(tensor_peers)
    ]
    low[my_half, my_rows, :] = own2[...]

    for copy in step1:
        copy.wait_recv()
    of_x, of_up, of_down = x_next, y_up, y_down
    step2 = [
        send_x(of_x, high_half, 5, y_up),
        send_x(of_x, high_half, 6, y_down),
        send_x(of_up, low_half, 3, x_next),
        send_x(of_down, low_half, 4, x_next),
        send_x(of_down, low_half, 7, y_up),
        send_x(of_up, high_half, 8, y_down),
    ]
    shared += [share_x(of_x, 1), share_x(of_up, 2), share_x(of_down, 3)]

    for copy in copies2:
        copy.wait_recv()

    low0, low1 = low[0], low[1]
    grad_a[...] = dot(xt[:, 0:256], low0, 1, 1) + dot(xt[:, 256:512], low1, 1, 1)
    msg3a[...] = jnp.where(left, pltpu.roll(grad_a[0:160, :], RANK, 1), grad_a[160:320, :]).astype(BF)
    copies3a = [remote(msg3a, got3a.at[g], s3a, r3a, k, gg, t) for k, gg in enumerate(group_peers)]
    got3a[g] = msg3a[...]

    def grad_rows(i, carry):
        rows = aligned(i, 400)
        grad_b[rows, :] = dot(cot[rows, 0:256], low0, 1, 1) + dot(cot[rows, 256:512], low1, 1, 1)
        return carry

    lax.fori_loop(0, HID // 400, grad_rows, 0)

    def message3(j):
        return beside(
            grad_b[pl.ds(pl.multiple_of(j * SHARE_B, 8), 112), :],
            grad_b[pl.ds(pl.multiple_of(j * SHARE_B + 104, 8), 112), :],
        ).astype(BF)

    copies3b = []
    for k, gg in enumerate(group_peers):
        msg3b[k] = message3(gg)
        copies3b.append(remote(msg3b.at[k], got3b.at[g], s3b, r3b, k, gg, t))
    got3b[g] = message3(g)

    for copy in copies0b:
        copy.wait_recv()

    def packed_right(rows):
        return jnp.where(left, pltpu.roll(rows[0:160], RANK, 1), rows[160:320])

    master_a = packed_right(mom_a[0])
    second_a = packed_right(mom_a[1])
    first_a = beside(mom_a[0, 0:160, :], mom_a[0, 160:320, :])

    for copy in step2:
        copy.wait_recv()
    across = tensor_at(0, 2, 0)
    quarter = D // 4
    step3 = [
        send_x(across, low_half, 9, x_next),
        send_x(tensor_at(1, 1, 0), pl.ds(2 * quarter, quarter), 10, y_down),
        send_x(tensor_at(1, 3, 0), pl.ds(3 * quarter, quarter), 11, y_up),
    ]
    shared += [share_x(across, 4), share_x(tensor_at(1, 1, 0), 5), share_x(tensor_at(1, 3, 0), 6)]

    def base_rows(h, first, last):
        tokens = aligned(h, 256)

        def body(i, carry):
            rows = aligned(i, 800)
            acc[h, rows, :] = dot(base[rows, :], xall[tokens, :], 1, 1)
            return carry

        lax.fori_loop(first, last, body, 0)

    def adam(master, first, second, got):
        grad = got[0].astype(F32)
        for j in range(1, NG):
            grad = grad + got[j].astype(F32)
        grad = adapter_scale * grad
        first_next = beta_one * first + (1.0 - beta_one) * grad
        second_next = beta_two * second + (1.0 - beta_two) * grad * grad
        master_next = master - learn_rate * (first_next / fix_one) / (
            jnp.sqrt(second_next / fix_two) + adam_eps
        )
        return master_next, first_next, second_next

    load_base.wait()
    for k in (0, 2, 3, 4):
        shared[k].wait_recv()
    base_rows(xl, 0, 1)

    for copy in copies3a:
        copy.wait_recv()
    next_a = adam(master_a, first_a, second_a, got3a)
    new_a = next_a[0].astype(BF).astype(F32)
    turned = pltpu.roll(new_a, RANK, 1)
    place = pl.multiple_of(core * RANK, RANK)
    a_left[pl.ds(place, 160), :] = jnp.where(left, new_a, 0.0).astype(BF)
    a_left[pl.ds(place + 160, 160), :] = jnp.where(left, turned, 0.0).astype(BF)
    a_right[pl.ds(place, 160), :] = jnp.where(left, 0.0, turned).astype(BF)
    a_right[pl.ds(place + 160, 160), :] = jnp.where(left, 0.0, new_a).astype(BF)

    for k in (1, 5, 6):
        shared[k].wait_recv()
    for copy in early:
        copy.wait_recv()
    own_window = window_of(t)
    for dx in range(2):
        for dy in range(4):
            for dc in range(2):
                rows = aligned(tensor_at(dx, dy, dc), ROWS)
                window_x[rows, :] = cross[dc] if (dx, dy) == (1, 2) else xall[rows, own_window]
    part5[...] = (
        dot(window_x[0:256, :], a_left[...], 1, 0) + dot(window_x[256:512, :], a_right[...], 1, 0)
    ).astype(BF)
    copies5 = [
        remote(part5.at[aligned(tt, 16)], got5.at[k], s5, r5, k, g, tt)
        for k, tt in enumerate(tensor_peers)
    ]

    for copy in copies3b:
        copy.wait_recv()
    next_b = adam(mom_b[0], mom_b[1], mom_b[2], got3b)
    msg4[...] = next_b[0].astype(BF)
    copies4 = [remote(msg4, got4.at[g], s4, r4, k, gg, t) for k, gg in enumerate(group_peers)]
    got4[g] = msg4[...]

    for copy in step3:
        copy.wait_recv()
    shared.append(share_x(tensor_at(1, 2, 0), 7))

    base_rows(xl, 1, 2)

    for copy in copies5:
        copy.wait_recv()
    mine5 = aligned(t, 16)
    total = part5[mine5, :].astype(F32)
    for k in range(NT - 1):
        total = total + got5[k].astype(F32)
    own5[...] = (adapter_scale * total).astype(BF)
    copies6 = [remote(own5, xa.at[mine5], s6, r6, k, g, tt) for k, tt in enumerate(tensor_peers)]
    xa[mine5, :] = own5[...]

    shared[7].wait_recv()
    base_rows(1 - xl, 0, 2)

    rows_out = aligned(lax.rem(g, 4), SHARE_A)
    for i in range(3):
        grad_a[0:160, :] = next_a[i]
        own_rows = grad_a[rows_out, :]
        own_rows = jnp.where(g < 4, own_rows, pltpu.roll(own_rows, RANK, 1))
        a_state[i] = own_rows[:, 0:RANK]
        rows_b[0:104, :] = next_b[i][0:104]
        rows_b[104:200, :] = pltpu.roll(next_b[i], RANK, 1)[0:96]
        b_state[i, :, 0, 0:128] = rows_b[0:128, :].T[0:RANK]
        b_state[i, :, 0, 128:SHARE_B] = rows_b[128:256, :].T[0:RANK, 0:SHARE_B - 128]

    for copy in copies4:
        copy.wait_recv()
    for j in range(NG):
        rows = got4[j].astype(F32)
        b_rows[j * SHARE_B:j * SHARE_B + 104, :] = jnp.where(left[0:104], rows[0:104], 0.0)
        b_rows[j * SHARE_B + 104:(j + 1) * SHARE_B, :] = jnp.where(
            left[0:96], pltpu.roll(rows, RANK, 1)[0:96], 0.0
        )
    b_left[...] = b_rows[...].astype(BF)
    b_right[...] = pltpu.roll(b_rows[...], RANK, 1).astype(BF)

    for copy in copies6:
        copy.wait_recv()
    for group in (
        copies0, step1, shared, early, copies0b, copies1, step2, copies2, copies3a, copies3b, step3, copies4, copies5, copies6,
    ):
        for copy in group:
            copy.wait_send()


def finish(
    acc, b_left, b_right, xa, a_state, b_state,
    out_hbm, ma_out, m1a_out, m2a_out, mb_out, m1b_out, m2b_out,
    out_v, sem,
):
    def store(src, dst, k):
        copy = pltpu.make_async_copy(src, dst, sem.at[k])
        copy.start()
        return copy

    stores = []
    for i in range(5):
        rows = pl.ds(320 * i, 320)
        out_v[rows, 0:256] = (acc[0, rows, :] + dot(b_left[rows, :], xa[...], 1, 1)).astype(BF)
        out_v[rows, 256:512] = (acc[1, rows, :] + dot(b_right[rows, :], xa[...], 1, 1)).astype(BF)
        stores.append(store(out_v.at[rows], out_hbm.at[rows], i))
        if i == 0:
            stores += [store(a_state.at[j], ref, 5 + j) for j, ref in enumerate((ma_out, m1a_out, m2a_out))]
            stores += [store(b_state.at[j], ref, 8 + j) for j, ref in enumerate((mb_out, m1b_out, m2b_out))]
    for copy in stores:
        copy.wait()


def shards(
    frozen_base_matrix, master_a, moment1_a, moment2_a, master_b, moment1_b, moment2_b,
    learner_token_inputs, learner_output_cotangents, rollout_inputs,
):
    state_a = [ref.reshape(RANK, SHARE_A).T for ref in (master_a, moment1_a, moment2_a)]
    dma = pltpu.SemaphoreType.DMA
    vmem = pltpu.VMEM
    any_space = pl.BlockSpec(memory_space=pl.ANY)
    in_vmem = pl.BlockSpec(memory_space=pltpu.VMEM)
    shape = jax.ShapeDtypeStruct
    mib = 1024 * 1024
    operands = (
        frozen_base_matrix.T, *state_a, master_b, moment1_b, moment2_b,
        learner_token_inputs.T, learner_output_cotangents.T, rollout_inputs,
    )
    parts = pl.pallas_call(
        kernel,
        out_shape=[
            vmem((2, HID, 256), F32),
            vmem((HID, 128), BF),
            vmem((HID, 128), BF),
            vmem((256, 128), BF),
            vmem((3, SHARE_A, RANK), F32),
            vmem((3, RANK, 1, SHARE_B), F32),
        ],
        in_specs=[any_space] * 10,
        out_specs=[in_vmem] * 6,
        scratch_shapes=[
            vmem((HID, D), BF),
            vmem((COLS, TOK), BF),
            vmem((HID, TOK), BF),
            vmem((TOK, D), BF),
            vmem((3, SHARE_A, RANK), F32),
            vmem((3, RANK, 1, SHARE_B), F32),
            vmem((3, 128, 128), F32),
            vmem((RANK, 256), BF),
            vmem((NG, RANK, 256), BF),
            vmem((2, SHARE_A, 128), F32),
            vmem((2, COLS, 128), F32),
            vmem((3, 112, 128), F32),
            vmem((RANK, COLS), BF),
            vmem((RANK, HID), BF),
            vmem((2, 128, 256), BF),
            vmem((NT - 1, 16, 256), BF),
            vmem((2, 128, 256), BF),
            vmem((16, 256), BF),
            vmem((HID + 16, 128), F32),
            vmem((COLS, 128), F32),
            vmem((160, 128), BF),
            vmem((NG, 160, 128), BF),
            vmem((NG - 1, 112, 128), BF),
            vmem((NG, 112, 128), BF),
            vmem((112, 128), BF),
            vmem((NG, 112, 128), BF),
            vmem((HID, 128), F32),
            vmem((256, 128), F32),
            vmem((384, 128), BF),
            vmem((384, 128), BF),
            vmem((2, ROWS, 384), BF),
            vmem((TOK, 384), BF),
            vmem((256, 128), BF),
            vmem((NT - 1, 16, 128), BF),
            vmem((16, 128), BF),
            dma((10,)),
        ]
        + [dma((n,)) for n in (7, 7, 7, 7, 15, 15, 15, 15, 7, 7, 7, 7, 7, 7, 15, 15, 15, 15, 12, 12, 8, 8, 2, 2)],
        compiler_params=pltpu.CompilerParams(
            collective_id=0, has_side_effects=True, vmem_limit_bytes=44 * mib
        ),
        cost_estimate=pl.CostEstimate(
            flops=2 * TOK * D * HID, bytes_accessed=2 * (D * HID + 2 * TOK * HID), transcendentals=0
        ),
    )(*[pltpu.with_memory_space_constraint(operand, pltpu.HBM) for operand in operands])
    results = pl.pallas_call(
        finish,
        out_shape=[shape((HID, TOK), BF)]
        + [shape((SHARE_A, RANK), F32)] * 3
        + [shape((RANK, 1, SHARE_B), F32)] * 3,
        in_specs=[in_vmem] * 6,
        out_specs=[any_space] * 7,
        scratch_shapes=[vmem((HID, TOK), BF), dma((11,))],
        compiler_params=pltpu.CompilerParams(vmem_limit_bytes=10 * mib),
        cost_estimate=pl.CostEstimate(
            flops=2 * TOK * RANK * HID, bytes_accessed=2 * TOK * HID, transcendentals=0
        ),
    )(*parts)
    out, a_next, b_next = results[0], results[1:4], results[4:7]
    return (out.T, *[ref.T.reshape(RANK, 1, SHARE_A) for ref in a_next], *b_next)


def solution(mesh):
    state = P(None, "tensor", "group")
    return jax.shard_map(
        shards,
        mesh=mesh,
        in_specs=(P(None, "tensor"), *[state] * 6, P("group", "tensor"), P("group", "tensor"), P(("group", "tensor"), None)),
        out_specs=(P("group", "tensor"), *[state] * 6),
        check_vma=False,
    )
```

time: 71 us -> 57.8 us (0.81)
  Pallas kernels: 63.7 us -> 56.8 us
  local copies, waits for them, and re-layouts: 6.49 us -> 0 us
    pallas_call x1 -> x2, Pallas kernels: 63.7 us -> 56.8 us  [the longest x1 55.2 us: shards(): pl.pallas_call(kernel, out_shape=[vmem((2, HID, 256), F32), vmem((HID, 12...]
    unnamed x19 -> x0, local copies, waits for them, and re-layouts: 6.49 us -> none
where the time goes in v2:
time: 57.8 us; the launch traced here: 57.5 us
  Pallas kernels  56.8 us (98%)
  between operations  0.64 us (1%)
    pallas_call x1, Pallas kernels, shards(): pl.pallas_call(kernel, out_shape=[vmem((2, HID, 256), F32), vmem((HID, 12...  55.2 us
    pallas_call x1, Pallas kernels, shards(): pl.pallas_call(finish, out_shape=[shape((HID, TOK), BF)] + [shape((SHARE_...  1.59 us

profile of v2, /device:TPU:1, one launch (start us, length us, event | category | flops | bytes accessed | tf_op | source)
XLA Modules:
  0.0 57.5 jit_solution(11697086904116050634)
XLA Ops:
  0.6 55.2 %shard_map.153 = (f32[2,1600,256]{2,1,0:T(8,128)S(1)}, bf16[1600,128]{1,0:T(8,128)(2,1)S(1)}, bf16[1600,128]{1,0:T(8,128)(2,1)S(1)}, bf16[256,128]{1,0:T(8,128)(...) custom-call(bf16[1600,5120]{1,0:T(8,128)(2,1)} %bitcast.22, f32[40,64]{1,0:T(8,128)} %bitcast.26, ...), custom_call_target="tpu_custom_call" | custom-call | flops 8388608000 | bytes 19660800 | tf_op jit(solution)/shard_map/pallas_call | solution.py:403
  55.9 1.6 %shard_map.154 = (bf16[1600,512]{1,0:T(8,128)(2,1)}, f32[40,64]{1,0:T(8,128)}, f32[40,64]{1,0:T(8,128)}, f32[40,64]{1,0:T(8,128)}, f32[64,1,200]{2,1,0:T(1,128)}...) custom-call(f32[2,1600,256]{2,1,0:T(8,128)S(1)} %get-tuple-element.20.acc, ...), custom_call_target="tpu_custom_call" | custom-call | flops 104857600 | bytes 1638400 | tf_op jit(solution)/shard_map/pallas_call | solution.py:461

commit v3 on v2

--- a/solution.py
+++ b/solution.py
@@ -84,7 +84,16 @@
 
     load_b = load(mb_hbm, b_in.at[0], 0)
     load_a = load(ma_hbm, a_in.at[0], 1)
-    mine = aligned(t, ROWS)
+
+    def slot(at_y, dx, dy):
+        place = lax.rem(at_y + (2 if (dx, dy) == (1, 0) or (dx, dy) == (0, 2) else 0) + dy, 4)
+        late = (dx, dy) == (0, 2) or (dx == 1 and dy != 0)
+        return (8 if late else 0) + place * 2
+
+    def rows_of(dx, dy, at_core=core, at_y=y):
+        return aligned(slot(at_y, dx, dy) + at_core, ROWS)
+
+    mine = rows_of(0, 0)
     load_x = load(xr_hbm, xall.at[mine], 2)
     load_cot = load(cot_hbm, cot, 3)
     load_xt = load(xt_hbm, xt, 4)
@@ -107,27 +116,46 @@
     got0[g] = msg0[...]
 
     x_next, y_up, y_down, sibling = tensor_at(1, 0, 0), tensor_at(0, 1, 0), tensor_at(0, 3, 0), tensor_at(0, 0, 1)
-    half = D // 2
-    low_half, high_half, all_of = pl.ds(0, half), pl.ds(half, half), pl.ds(0, D)
-
-    def send_x(owner, columns, k, to):
-        where = xall.at[aligned(owner, ROWS), columns]
-        return remote(where, where, sx, rx, k, g, to)
-
-    def share_x(owner, k):
-        where = xall.at[aligned(owner, ROWS)]
-        return remote(where, where, sc, rc, k, g, sibling)
+    half, quarter = D // 2, D // 4
+    own_half, other_half = xl, 1 - xl
+    sent_x, sent_share = [], []
+
+    def columns_of(first, count=1):
+        return pl.ds(pl.multiple_of(first * quarter, quarter), count * quarter)
+
+    def half_of(i):
+        return pl.ds(pl.multiple_of(i * half, half), half)
+
+    def send_x(here, there, at_y, columns, to):
+        copy = remote(
+            xall.at[rows_of(*here), columns], xall.at[rows_of(*there, at_y=at_y), columns],
+            sx, rx, len(sent_x), g, to,
+        )
+        sent_x.append(copy)
+        return copy
+
+    def share_x(here, columns):
+        where = xall.at[rows_of(*here), columns]
+        copy = remote(where, where, sc, rc, len(sent_share), g, sibling)
+        sent_share.append(copy)
+        return copy
+
+    def arrived(copies):
+        for copy in copies:
+            copy.wait_recv()
+
+    everything = pl.ds(0, D)
 
     def window_of(tt):
         return pl.ds(pl.multiple_of((tt // 2) * 640 + lax.rem(tt, 2) * 256, 128), 384)
 
     load_x.wait()
-    step1 = [send_x(t, all_of, 0, x_next), send_x(t, all_of, 1, y_up), send_x(t, all_of, 2, y_down)]
-    shared = [share_x(t, 0)]
-    far_chip = [tensor_at(1, 2, 0), tensor_at(1, 2, 1)]
-    early = [
-        remote(xall.at[mine, window_of(tt)], cross.at[k], sw, rw, k, g, tt) for k, tt in enumerate(far_chip)
-    ]
+    step_a = [
+        send_x((0, 0), (0, 3), y + 1, columns_of(0, 3), y_up),
+        send_x((0, 0), (0, 1), y + 3, columns_of(1, 3), y_down),
+        send_x((0, 0), (1, 0), y, half_of(other_half), x_next),
+    ]
+    near = [share_x((0, 0), everything)]
 
     lanes = lax.broadcasted_iota(jnp.int32, (160, 128), 1)
     left = lanes < RANK
@@ -171,8 +199,16 @@
         for k, tt in enumerate(tensor_peers)
     ]
 
+    step_b = [
+        send_x((0, 0), (0, 3), y + 1, columns_of(3), y_up),
+        send_x((0, 0), (0, 1), y + 3, columns_of(0), y_down),
+        send_x((0, 0), (1, 0), y, half_of(own_half), x_next),
+    ]
+
+    partner = group_at(0, 1)
+    z_peers = [group_at(dz, 0) for dz in (2, 1, 3)]
     copies0b = [
-        remote(msg0b, mom_a.at[:, rows_a, :], s0b, r0b, k, gg, t) for k, gg in enumerate(group_peers)
+        remote(msg0b, mom_a.at[:, rows_a, :], s0b, r0b, k, gg, t) for k, gg in enumerate([partner] + z_peers)
     ]
 
     for copy in copies1:
@@ -187,18 +223,35 @@
     ]
     low[my_half, my_rows, :] = own2[...]
 
-    for copy in step1:
-        copy.wait_recv()
-    of_x, of_up, of_down = x_next, y_up, y_down
-    step2 = [
-        send_x(of_x, high_half, 5, y_up),
-        send_x(of_x, high_half, 6, y_down),
-        send_x(of_up, low_half, 3, x_next),
-        send_x(of_down, low_half, 4, x_next),
-        send_x(of_down, low_half, 7, y_up),
-        send_x(of_up, high_half, 8, y_down),
-    ]
-    shared += [share_x(of_x, 1), share_x(of_up, 2), share_x(of_down, 3)]
+    arrived(step_a)
+    early = []
+    for dy in (2, 1, 3):
+        for dc in range(2):
+            to = tensor_at(0, dy, dc)
+            k = 2 * (dy - 1) + dc
+            early.append(
+                remote(xall.at[rows_of(1, 0), window_of(to)], cross.at[k], sw, rw, k, g, to)
+            )
+    step_c = [
+        send_x((0, 3), (0, 2), y + 1, columns_of(0, 2), y_up),
+        send_x((0, 1), (0, 2), y + 3, columns_of(2, 2), y_down),
+    ]
+    step_d = [
+        send_x((1, 0), (1, 3), y + 1, half_of(own_half), y_up),
+        send_x((1, 0), (1, 1), y + 3, half_of(own_half), y_down),
+    ]
+    step_e = [
+        send_x((0, 1), (1, 1), y, columns_of(2 * own_half + 1), x_next),
+        send_x((0, 3), (1, 3), y, columns_of(2 * own_half), x_next),
+    ]
+    arrived(step_b)
+    near += [share_x(there, everything) for there in ((1, 0), (0, 1), (0, 3))]
+    copies0b[0].wait_recv()
+    rows_partner = aligned(partner, SHARE_A)
+    copies0b += [
+        remote(mom_a.at[:, rows_partner, :], mom_a.at[:, rows_partner, :], s0b, r0b, 4 + k, gg, t)
+        for k, gg in enumerate(z_peers)
+    ]
 
     for copy in copies2:
         copy.wait_recv()
@@ -228,8 +281,7 @@
         copies3b.append(remote(msg3b.at[k], got3b.at[g], s3b, r3b, k, gg, t))
     got3b[g] = message3(g)
 
-    for copy in copies0b:
-        copy.wait_recv()
+    arrived(copies0b[1:])
 
     def packed_right(rows):
         return jnp.where(left, pltpu.roll(rows[0:160], RANK, 1), rows[160:320])
@@ -238,26 +290,20 @@
     second_a = packed_right(mom_a[1])
     first_a = beside(mom_a[0, 0:160, :], mom_a[0, 160:320, :])
 
-    for copy in step2:
-        copy.wait_recv()
-    across = tensor_at(0, 2, 0)
-    quarter = D // 4
-    step3 = [
-        send_x(across, low_half, 9, x_next),
-        send_x(tensor_at(1, 1, 0), pl.ds(2 * quarter, quarter), 10, y_down),
-        send_x(tensor_at(1, 3, 0), pl.ds(3 * quarter, quarter), 11, y_up),
-    ]
-    shared += [share_x(across, 4), share_x(tensor_at(1, 1, 0), 5), share_x(tensor_at(1, 3, 0), 6)]
-
-    def base_rows(h, first, last):
-        tokens = aligned(h, 256)
-
+    def base_rows(part, first, last):
         def body(i, carry):
             rows = aligned(i, 800)
-            acc[h, rows, :] = dot(base[rows, :], xall[tokens, :], 1, 1)
+            acc[part, rows, :] = dot(base[rows, :], xall[part * 256:(part + 1) * 256, :], 1, 1)
             return carry
 
         lax.fori_loop(first, last, body, 0)
+
+    load_base.wait()
+    arrived(near)
+    base_rows(0, 0, 1)
+
+    arrived(step_c)
+    two_away = share_x((0, 2), everything)
 
     def adam(master, first, second, got):
         grad = got[0].astype(F32)
@@ -271,11 +317,6 @@
         )
         return master_next, first_next, second_next
 
-    load_base.wait()
-    for k in (0, 2, 3, 4):
-        shared[k].wait_recv()
-    base_rows(xl, 0, 1)
-
     for copy in copies3a:
         copy.wait_recv()
     next_a = adam(master_a, first_a, second_a, got3a)
@@ -287,16 +328,14 @@
     a_right[pl.ds(place, 160), :] = jnp.where(left, 0.0, turned).astype(BF)
     a_right[pl.ds(place + 160, 160), :] = jnp.where(left, 0.0, new_a).astype(BF)
 
-    for k in (1, 5, 6):
-        shared[k].wait_recv()
-    for copy in early:
-        copy.wait_recv()
+    arrived(early + [two_away])
     own_window = window_of(t)
     for dx in range(2):
         for dy in range(4):
             for dc in range(2):
                 rows = aligned(tensor_at(dx, dy, dc), ROWS)
-                window_x[rows, :] = cross[dc] if (dx, dy) == (1, 2) else xall[rows, own_window]
+                held = rows_of(dx, dy, lax.rem(core + dc, 2))
+                window_x[rows, :] = cross[2 * ((4 - dy) - 1) + dc] if dx == 1 and dy else xall[held, own_window]
     part5[...] = (
         dot(window_x[0:256, :], a_left[...], 1, 0) + dot(window_x[256:512, :], a_right[...], 1, 0)
     ).astype(BF)
@@ -305,6 +344,12 @@
         for k, tt in enumerate(tensor_peers)
     ]
 
+    step_f = [
+        send_x((1, 0), (1, 3), y + 1, columns_of(2 * other_half + 1), y_up),
+        send_x((1, 0), (1, 1), y + 3, columns_of(2 * other_half), y_down),
+        send_x((0, 2), (1, 2), y, half_of(own_half), x_next),
+    ]
+
     for copy in copies3b:
         copy.wait_recv()
     next_b = adam(mom_b[0], mom_b[1], mom_b[2], got3b)
@@ -312,11 +357,14 @@
     copies4 = [remote(msg4, got4.at[g], s4, r4, k, gg, t) for k, gg in enumerate(group_peers)]
     got4[g] = msg4[...]
 
-    for copy in step3:
-        copy.wait_recv()
-    shared.append(share_x(tensor_at(1, 2, 0), 7))
-
-    base_rows(xl, 1, 2)
+    arrived(step_d + step_e)
+    step_g = [
+        send_x((1, 1), (1, 2), y + 3, columns_of(2 * own_half), y_down),
+        send_x((1, 3), (1, 2), y + 1, columns_of(2 * own_half + 1), y_up),
+    ]
+    away = [share_x(there, half_of(own_half)) for there in ((1, 1), (1, 3))]
+
+    base_rows(0, 1, 2)
 
     for copy in copies5:
         copy.wait_recv()
@@ -328,8 +376,10 @@
     copies6 = [remote(own5, xa.at[mine5], s6, r6, k, g, tt) for k, tt in enumerate(tensor_peers)]
     xa[mine5, :] = own5[...]
 
-    shared[7].wait_recv()
-    base_rows(1 - xl, 0, 2)
+    arrived(step_f + step_g)
+    away += [share_x((1, 2), everything)] + [share_x(there, half_of(other_half)) for there in ((1, 1), (1, 3))]
+    arrived(away)
+    base_rows(1, 0, 2)
 
     rows_out = aligned(lax.rem(g, 4), SHARE_A)
     for i in range(3):
@@ -356,7 +406,7 @@
     for copy in copies6:
         copy.wait_recv()
     for group in (
-        copies0, step1, shared, early, copies0b, copies1, step2, copies2, copies3a, copies3b, step3, copies4, copies5, copies6,
+        copies0, sent_x, sent_share, early, copies0b, copies1, copies2, copies3a, copies3b, copies4, copies5, copies6,
     ):
         for copy in group:
             copy.wait_send()
@@ -372,11 +422,18 @@
         copy.start()
         return copy
 
+    t = lax.axis_index("tensor")
+    xl, y = t // 8, lax.rem(t // 2, 4)
+    place = lax.broadcasted_iota(jnp.int32, (320, 256), 1) // 64
+    from_late, from_early = place == lax.rem(y + 2, 4), place == y
     stores = []
     for i in range(5):
         rows = pl.ds(320 * i, 320)
-        out_v[rows, 0:256] = (acc[0, rows, :] + dot(b_left[rows, :], xa[...], 1, 1)).astype(BF)
-        out_v[rows, 256:512] = (acc[1, rows, :] + dot(b_right[rows, :], xa[...], 1, 1)).astype(BF)
+        near, away = acc[0, rows, :], acc[1, rows, :]
+        own = jnp.where(from_late, jnp.concatenate([away[:, 128:], away[:, :128]], axis=1), near)
+        other = jnp.where(from_early, jnp.concatenate([near[:, 128:], near[:, :128]], axis=1), away)
+        out_v[rows, 0:256] = (jnp.where(xl == 0, own, other) + dot(b_left[rows, :], xa[...], 1, 1)).astype(BF)
+        out_v[rows, 256:512] = (jnp.where(xl == 0, other, own) + dot(b_right[rows, :], xa[...], 1, 1)).astype(BF)
         stores.append(store(out_v.at[rows], out_hbm.at[rows], i))
         if i == 0:
             stores += [store(a_state.at[j], ref, 5 + j) for j, ref in enumerate((ma_out, m1a_out, m2a_out))]
@@ -443,14 +500,14 @@
             vmem((256, 128), F32),
             vmem((384, 128), BF),
             vmem((384, 128), BF),
-            vmem((2, ROWS, 384), BF),
+            vmem((6, ROWS, 384), BF),
             vmem((TOK, 384), BF),
             vmem((256, 128), BF),
             vmem((NT - 1, 16, 128), BF),
             vmem((16, 128), BF),
             dma((10,)),
         ]
-        + [dma((n,)) for n in (7, 7, 7, 7, 15, 15, 15, 15, 7, 7, 7, 7, 7, 7, 15, 15, 15, 15, 12, 12, 8, 8, 2, 2)],
+        + [dma((n,)) for n in (7, 7, 7, 7, 15, 15, 15, 15, 7, 7, 7, 7, 7, 7, 15, 15, 15, 15, 17, 17, 10, 10, 6, 6)],
         compiler_params=pltpu.CompilerParams(
             collective_id=0, has_side_effects=True, vmem_limit_bytes=44 * mib
         ),

time: 57.8 us -> 52.5 us (0.908)
  Pallas kernels: 56.8 us -> 51.7 us
    pallas_call x1, Pallas kernels: 55.2 us -> 50.1 us  [shards(): pl.pallas_call(kernel, out_shape=[vmem((2, HID, 256), F32), vmem((HID, 12...]
where the time goes in v3:
time: 52.5 us; the launch traced here: 52.4 us
  Pallas kernels  51.7 us (98%)
  between operations  0.64 us (1%)
    pallas_call x1, Pallas kernels, shards(): pl.pallas_call(kernel, out_shape=[vmem((2, HID, 256), F32), vmem((HID, 12...  50.1 us
    pallas_call x1, Pallas kernels, shards(): pl.pallas_call(finish, out_shape=[shape((HID, TOK), BF)] + [shape((SHARE_...  1.59 us

profile of v3, /device:TPU:1, one launch (start us, length us, event | category | flops | bytes accessed | tf_op | source)
XLA Modules:
  0.0 52.4 jit_solution(8233181774338278310)
XLA Ops:
  0.6 50.1 %shard_map.153 = (f32[2,1600,256]{2,1,0:T(8,128)S(1)}, bf16[1600,128]{1,0:T(8,128)(2,1)S(1)}, bf16[1600,128]{1,0:T(8,128)(2,1)S(1)}, bf16[256,128]{1,0:T(8,128)(...) custom-call(bf16[1600,5120]{1,0:T(8,128)(2,1)} %bitcast.22, f32[40,64]{1,0:T(8,128)} %bitcast.26, ...), custom_call_target="tpu_custom_call" | custom-call | flops 8388608000 | bytes 19660800 | tf_op jit(solution)/shard_map/pallas_call | solution.py:460
  50.8 1.6 %shard_map.154 = (bf16[1600,512]{1,0:T(8,128)(2,1)}, f32[40,64]{1,0:T(8,128)}, f32[40,64]{1,0:T(8,128)}, f32[40,64]{1,0:T(8,128)}, f32[64,1,200]{2,1,0:T(1,128)}...) custom-call(f32[2,1600,256]{2,1,0:T(8,128)S(1)} %get-tuple-element.20.acc, ...), custom_call_target="tpu_custom_call" | custom-call | flops 104857600 | bytes 1638400 | tf_op jit(solution)/shard_map/pallas_call | solution.py:518

commit v4 on v3

--- a/solution.py
+++ b/solution.py
@@ -146,14 +146,21 @@
 
     everything = pl.ds(0, D)
 
+    def base_part(part, columns):
+        tokens = xall[part * 256:(part + 1) * 256, columns]
+        for rows in (pl.ds(0, 800), pl.ds(800, 800)):
+            acc[part, rows, :] += dot(base[rows, columns], tokens, 1, 1)
+
     def window_of(tt):
         return pl.ds(pl.multiple_of((tt // 2) * 640 + lax.rem(tt, 2) * 256, 128), 384)
 
     load_x.wait()
     step_a = [
-        send_x((0, 0), (0, 3), y + 1, columns_of(0, 3), y_up),
-        send_x((0, 0), (0, 1), y + 3, columns_of(1, 3), y_down),
+        send_x((0, 0), (0, 3), y + 1, half_of(own_half), y_up),
+        send_x((0, 0), (0, 1), y + 3, half_of(own_half), y_down),
         send_x((0, 0), (1, 0), y, half_of(other_half), x_next),
+        send_x((0, 0), (0, 3), y + 1, columns_of(2 * other_half), y_up),
+        send_x((0, 0), (0, 1), y + 3, columns_of(2 * other_half + 1), y_down),
     ]
     near = [share_x((0, 0), everything)]
 
@@ -174,6 +181,7 @@
         mom_b[i] = beside(rows_b[0:112, :], rows_b[104:216, :])
     a_left[...] = jnp.zeros_like(a_left)
     a_right[...] = jnp.zeros_like(a_right)
+    acc[...] = jnp.zeros_like(acc)
     grad_b[HID:HID + 16, :] = jnp.zeros((16, 128), F32)
     msg0b[...] = jnp.zeros_like(msg0b)
     msg0b[0, :, 0:RANK] = a_in[1]
@@ -200,8 +208,8 @@
     ]
 
     step_b = [
-        send_x((0, 0), (0, 3), y + 1, columns_of(3), y_up),
-        send_x((0, 0), (0, 1), y + 3, columns_of(0), y_down),
+        send_x((0, 0), (0, 3), y + 1, columns_of(2 * other_half + 1), y_up),
+        send_x((0, 0), (0, 1), y + 3, columns_of(2 * other_half), y_down),
         send_x((0, 0), (1, 0), y, half_of(own_half), x_next),
     ]
 
@@ -233,8 +241,10 @@
                 remote(xall.at[rows_of(1, 0), window_of(to)], cross.at[k], sw, rw, k, g, to)
             )
     step_c = [
-        send_x((0, 3), (0, 2), y + 1, columns_of(0, 2), y_up),
-        send_x((0, 1), (0, 2), y + 3, columns_of(2, 2), y_down),
+        send_x((0, 3), (0, 2), y + 1, columns_of(2 * own_half), y_up),
+        send_x((0, 1), (0, 2), y + 3, columns_of(2 * own_half + 1), y_down),
+        send_x((0, 3), (0, 2), y + 1, columns_of(2 * other_half), y_up),
+        send_x((0, 1), (0, 2), y + 3, columns_of(2 * other_half + 1), y_down),
     ]
     step_d = [
         send_x((1, 0), (1, 3), y + 1, half_of(own_half), y_up),
@@ -244,8 +254,13 @@
         send_x((0, 1), (1, 1), y, columns_of(2 * own_half + 1), x_next),
         send_x((0, 3), (1, 3), y, columns_of(2 * own_half), x_next),
     ]
+    near += [share_x(there, half_of(own_half)) for there in ((1, 0), (0, 1), (0, 3))]
     arrived(step_b)
-    near += [share_x(there, everything) for there in ((1, 0), (0, 1), (0, 3))]
+    near_b = [share_x(there, half_of(other_half)) for there in ((1, 0), (0, 1), (0, 3))]
+    step_d += [
+        send_x((1, 0), (1, 3), y + 1, columns_of(2 * other_half + 1), y_up),
+        send_x((1, 0), (1, 1), y + 3, columns_of(2 * other_half), y_down),
+    ]
     copies0b[0].wait_recv()
     rows_partner = aligned(partner, SHARE_A)
     copies0b += [
@@ -290,20 +305,21 @@
     second_a = packed_right(mom_a[1])
     first_a = beside(mom_a[0, 0:160, :], mom_a[0, 160:320, :])
 
-    def base_rows(part, first, last):
-        def body(i, carry):
-            rows = aligned(i, 800)
-            acc[part, rows, :] = dot(base[rows, :], xall[part * 256:(part + 1) * 256, :], 1, 1)
-            return carry
-
-        lax.fori_loop(first, last, body, 0)
-
     load_base.wait()
     arrived(near)
-    base_rows(0, 0, 1)
+    base_part(0, half_of(own_half))
 
     arrived(step_c)
     two_away = share_x((0, 2), everything)
+    step_f = [send_x((0, 2), (1, 2), y, columns_of(2 * other_half), x_next)]
+    arrived(early + [two_away])
+    own_window = window_of(t)
+    for dx in range(2):
+        for dy in range(4):
+            for dc in range(2):
+                rows = aligned(tensor_at(dx, dy, dc), ROWS)
+                held = rows_of(dx, dy, lax.rem(core + dc, 2))
+                window_x[rows, :] = cross[2 * ((4 - dy) - 1) + dc] if dx == 1 and dy else xall[held, own_window]
 
     def adam(master, first, second, got):
         grad = got[0].astype(F32)
@@ -328,14 +344,6 @@
     a_right[pl.ds(place, 160), :] = jnp.where(left, 0.0, turned).astype(BF)
     a_right[pl.ds(place + 160, 160), :] = jnp.where(left, 0.0, new_a).astype(BF)
 
-    arrived(early + [two_away])
-    own_window = window_of(t)
-    for dx in range(2):
-        for dy in range(4):
-            for dc in range(2):
-                rows = aligned(tensor_at(dx, dy, dc), ROWS)
-                held = rows_of(dx, dy, lax.rem(core + dc, 2))
-                window_x[rows, :] = cross[2 * ((4 - dy) - 1) + dc] if dx == 1 and dy else xall[held, own_window]
     part5[...] = (
         dot(window_x[0:256, :], a_left[...], 1, 0) + dot(window_x[256:512, :], a_right[...], 1, 0)
     ).astype(BF)
@@ -344,10 +352,11 @@
         for k, tt in enumerate(tensor_peers)
     ]
 
-    step_f = [
-        send_x((1, 0), (1, 3), y + 1, columns_of(2 * other_half + 1), y_up),
-        send_x((1, 0), (1, 1), y + 3, columns_of(2 * other_half), y_down),
-        send_x((0, 2), (1, 2), y, half_of(own_half), x_next),
+    arrived(step_e)
+    step_g = [
+        send_x((0, 2), (1, 2), y, columns_of(2 * other_half + 1), x_next),
+        send_x((1, 1), (1, 2), y + 3, columns_of(2 * other_half + 1), y_down),
+        send_x((1, 3), (1, 2), y + 1, columns_of(2 * other_half), y_up),
     ]
 
     for copy in copies3b:
@@ -357,15 +366,14 @@
     copies4 = [remote(msg4, got4.at[g], s4, r4, k, gg, t) for k, gg in enumerate(group_peers)]
     got4[g] = msg4[...]
 
-    arrived(step_d + step_e)
-    step_g = [
-        send_x((1, 1), (1, 2), y + 3, columns_of(2 * own_half), y_down),
-        send_x((1, 3), (1, 2), y + 1, columns_of(2 * own_half + 1), y_up),
-    ]
-    away = [share_x(there, half_of(own_half)) for there in ((1, 1), (1, 3))]
-
-    base_rows(0, 1, 2)
-
+    arrived(step_d + step_f)
+    away_a = [
+        share_x((1, 2), columns_of(2 * own_half)),
+        share_x((1, 1), everything),
+        share_x((1, 3), everything),
+    ]
+    arrived(near_b)
+    base_part(0, half_of(other_half))
     for copy in copies5:
         copy.wait_recv()
     mine5 = aligned(t, 16)
@@ -376,10 +384,8 @@
     copies6 = [remote(own5, xa.at[mine5], s6, r6, k, g, tt) for k, tt in enumerate(tensor_peers)]
     xa[mine5, :] = own5[...]
 
-    arrived(step_f + step_g)
-    away += [share_x((1, 2), everything)] + [share_x(there, half_of(other_half)) for there in ((1, 1), (1, 3))]
-    arrived(away)
-    base_rows(1, 0, 2)
+    arrived(step_g)
+    away_b = [share_x((1, 2), columns_of(2 * own_half + 1)), share_x((1, 2), half_of(other_half))]
 
     rows_out = aligned(lax.rem(g, 4), SHARE_A)
     for i in range(3):
@@ -403,6 +409,9 @@
     b_left[...] = b_rows[...].astype(BF)
     b_right[...] = pltpu.roll(b_rows[...], RANK, 1).astype(BF)
 
+    arrived(away_a + away_b)
+    base_part(1, half_of(own_half))
+    base_part(1, half_of(other_half))
     for copy in copies6:
         copy.wait_recv()
     for group in (
@@ -507,7 +516,7 @@
             vmem((16, 128), BF),
             dma((10,)),
         ]
-        + [dma((n,)) for n in (7, 7, 7, 7, 15, 15, 15, 15, 7, 7, 7, 7, 7, 7, 15, 15, 15, 15, 17, 17, 10, 10, 6, 6)],
+        + [dma((n,)) for n in (7, 7, 7, 7, 15, 15, 15, 15, 7, 7, 7, 7, 7, 7, 15, 15, 15, 15, 22, 22, 13, 13, 6, 6)],
         compiler_params=pltpu.CompilerParams(
             collective_id=0, has_side_effects=True, vmem_limit_bytes=44 * mib
         ),

time: 52.5 us -> 50.4 us (0.960)
  Pallas kernels: 51.7 us -> 49.6 us
    pallas_call x1, Pallas kernels: 50.1 us -> 48.1 us  [shards(): pl.pallas_call(kernel, out_shape=[vmem((2, HID, 256), F32), vmem((HID, 12...]
where the time goes in v4:
time: 50.4 us; the launch traced here: 50.3 us
  Pallas kernels  49.6 us (98%)
  between operations  0.64 us (1%)
    pallas_call x1, Pallas kernels, shards(): pl.pallas_call(kernel, out_shape=[vmem((2, HID, 256), F32), vmem((HID, 12...  48.1 us
    pallas_call x1, Pallas kernels, shards(): pl.pallas_call(finish, out_shape=[shape((HID, TOK), BF)] + [shape((SHARE_...  1.59 us

profile of v4, /device:TPU:1, one launch (start us, length us, event | category | flops | bytes accessed | tf_op | source)
XLA Modules:
  0.0 50.3 jit_solution(13714510935353598598)
XLA Ops:
  0.6 48.1 %shard_map.153 = (f32[2,1600,256]{2,1,0:T(8,128)S(1)}, bf16[1600,128]{1,0:T(8,128)(2,1)S(1)}, bf16[1600,128]{1,0:T(8,128)(2,1)S(1)}, bf16[256,128]{1,0:T(8,128)(...) custom-call(bf16[1600,5120]{1,0:T(8,128)(2,1)} %bitcast.22, f32[40,64]{1,0:T(8,128)} %bitcast.26, ...), custom_call_target="tpu_custom_call" | custom-call | flops 8388608000 | bytes 19660800 | tf_op jit(solution)/shard_map/pallas_call | solution.py:469
  48.7 1.6 %shard_map.154 = (bf16[1600,512]{1,0:T(8,128)(2,1)}, f32[40,64]{1,0:T(8,128)}, f32[40,64]{1,0:T(8,128)}, f32[40,64]{1,0:T(8,128)}, f32[64,1,200]{2,1,0:T(1,128)}...) custom-call(f32[2,1600,256]{2,1,0:T(8,128)S(1)} %get-tuple-element.20.acc, ...), custom_call_target="tpu_custom_call" | custom-call | flops 104857600 | bytes 1638400 | tf_op jit(solution)/shard_map/pallas_call | solution.py:527

commit v5 on v4

--- a/solution.py
+++ b/solution.py
@@ -312,6 +312,16 @@
     arrived(step_c)
     two_away = share_x((0, 2), everything)
     step_f = [send_x((0, 2), (1, 2), y, columns_of(2 * other_half), x_next)]
+    arrived(step_e)
+    step_g = [
+        send_x((0, 2), (1, 2), y, columns_of(2 * other_half + 1), x_next),
+        send_x((1, 1), (1, 2), y + 3, columns_of(2 * other_half + 1), y_down),
+        send_x((1, 3), (1, 2), y + 1, columns_of(2 * other_half), y_up),
+    ]
+
+    arrived(near_b)
+    base_part(0, half_of(other_half))
+
     arrived(early + [two_away])
     own_window = window_of(t)
     for dx in range(2):
@@ -352,13 +362,6 @@
         for k, tt in enumerate(tensor_peers)
     ]
 
-    arrived(step_e)
-    step_g = [
-        send_x((0, 2), (1, 2), y, columns_of(2 * other_half + 1), x_next),
-        send_x((1, 1), (1, 2), y + 3, columns_of(2 * other_half + 1), y_down),
-        send_x((1, 3), (1, 2), y + 1, columns_of(2 * other_half), y_up),
-    ]
-
     for copy in copies3b:
         copy.wait_recv()
     next_b = adam(mom_b[0], mom_b[1], mom_b[2], got3b)
@@ -372,20 +375,6 @@
         share_x((1, 1), everything),
         share_x((1, 3), everything),
     ]
-    arrived(near_b)
-    base_part(0, half_of(other_half))
-    for copy in copies5:
-        copy.wait_recv()
-    mine5 = aligned(t, 16)
-    total = part5[mine5, :].astype(F32)
-    for k in range(NT - 1):
-        total = total + got5[k].astype(F32)
-    own5[...] = (adapter_scale * total).astype(BF)
-    copies6 = [remote(own5, xa.at[mine5], s6, r6, k, g, tt) for k, tt in enumerate(tensor_peers)]
-    xa[mine5, :] = own5[...]
-
-    arrived(step_g)
-    away_b = [share_x((1, 2), columns_of(2 * own_half + 1)), share_x((1, 2), half_of(other_half))]
 
     rows_out = aligned(lax.rem(g, 4), SHARE_A)
     for i in range(3):
@@ -398,6 +387,21 @@
         b_state[i, :, 0, 0:128] = rows_b[0:128, :].T[0:RANK]
         b_state[i, :, 0, 128:SHARE_B] = rows_b[128:256, :].T[0:RANK, 0:SHARE_B - 128]
 
+    arrived(step_g)
+    away_b = [share_x((1, 2), columns_of(2 * own_half + 1)), share_x((1, 2), half_of(other_half))]
+    arrived(away_a + away_b[:1])
+    base_part(1, half_of(own_half))
+
+    for copy in copies5:
+        copy.wait_recv()
+    mine5 = aligned(t, 16)
+    total = part5[mine5, :].astype(F32)
+    for k in range(NT - 1):
+        total = total + got5[k].astype(F32)
+    own5[...] = (adapter_scale * total).astype(BF)
+    copies6 = [remote(own5, xa.at[mine5], s6, r6, k, g, tt) for k, tt in enumerate(tensor_peers)]
+    xa[mine5, :] = own5[...]
+
     for copy in copies4:
         copy.wait_recv()
     for j in range(NG):
@@ -409,8 +413,7 @@
     b_left[...] = b_rows[...].astype(BF)
     b_right[...] = pltpu.roll(b_rows[...], RANK, 1).astype(BF)
 
-    arrived(away_a + away_b)
-    base_part(1, half_of(own_half))
+    arrived(away_b[1:])
     base_part(1, half_of(other_half))
     for copy in copies6:
         copy.wait_recv()

time: 50.4 us -> 49.7 us (0.986)
  Pallas kernels: 49.6 us -> 48.9 us
    pallas_call x1, Pallas kernels: 48.1 us -> 47.4 us  [shards(): pl.pallas_call(kernel, out_shape=[vmem((2, HID, 256), F32), vmem((HID, 12...]
where the time goes in v5:
time: 49.7 us; the launch traced here: 49.6 us
  Pallas kernels  48.9 us (98%)
  between operations  0.64 us (1%)
    pallas_call x1, Pallas kernels, shards(): pl.pallas_call(kernel, out_shape=[vmem((2, HID, 256), F32), vmem((HID, 12...  47.4 us
    pallas_call x1, Pallas kernels, shards(): pl.pallas_call(finish, out_shape=[shape((HID, TOK), BF)] + [shape((SHARE_...  1.58 us

profile of v5, /device:TPU:1, one launch (start us, length us, event | category | flops | bytes accessed | tf_op | source)
XLA Modules:
  0.0 49.6 jit_solution(16998690507476191611)
XLA Ops:
  0.6 47.4 %shard_map.153 = (f32[2,1600,256]{2,1,0:T(8,128)S(1)}, bf16[1600,128]{1,0:T(8,128)(2,1)S(1)}, bf16[1600,128]{1,0:T(8,128)(2,1)S(1)}, bf16[256,128]{1,0:T(8,128)(...) custom-call(bf16[1600,5120]{1,0:T(8,128)(2,1)} %bitcast.22, f32[40,64]{1,0:T(8,128)} %bitcast.26, ...), custom_call_target="tpu_custom_call" | custom-call | flops 8388608000 | bytes 19660800 | tf_op jit(solution)/shard_map/pallas_call | solution.py:472
  48.0 1.6 %shard_map.154 = (bf16[1600,512]{1,0:T(8,128)(2,1)}, f32[40,64]{1,0:T(8,128)}, f32[40,64]{1,0:T(8,128)}, f32[40,64]{1,0:T(8,128)}, f32[64,1,200]{2,1,0:T(1,128)}...) custom-call(f32[2,1600,256]{2,1,0:T(8,128)S(1)} %get-tuple-element.20.acc, ...), custom_call_target="tpu_custom_call" | custom-call | flops 104857600 | bytes 1638400 | tf_op jit(solution)/shard_map/pallas_call | solution.py:530
